TPU v7x, 32 devices: a whole 2x2x4 slice. The times are simulated.
32 devices in a mesh: groups: 2 (over x), ranks: 8 (over z, y), tensor: 2 (over core).
Axes of the slice: x: 2, y: 2, z: 4, core: 2. Of those that a mesh axis runs over, the one named last changes fastest.
Arguments:
- hidden: bfloat16 [2048, 7168], P(('groups', 'ranks'), 'tensor'), parts along dimension 0, may hold values from -6 to 6
- w_down: bfloat16 [7168, 576], P('tensor'), may hold values from -0.0625 to 0.0625
- latent_gain: bfloat16 [512], replicated, may hold values from 0.099609375 to 1.8984375
- queries: bfloat16 [2048, 36864], P(('groups', 'ranks'), 'tensor'), parts along dimension 0, may hold values from -100 to 100
- w_up_value: bfloat16 [64, 512, 128], P('tensor', 'ranks'), may hold values from -0.25 to 0.25
- prompt_blocks: int32 [8], P('groups'), parts along dimension 0, may hold values from 1 to 4, 8 in all
- migrate: int32 [16, 8], P('groups'), parts along dimension 0, may hold values from 0 to 7, as said below
- owners: int32 [16, 8], P('groups'), parts along dimension 0, may hold values from 0 to 7, as said below
Outputs:
- served: bfloat16 [2048, 8192], P(('groups', 'ranks'), 'tensor'), parts along dimension 0
- cache_store: bfloat16 [2048, 576], P(('groups', 'ranks')), parts along dimension 0
There are 2 independent parts, one for each index of `groups`. A program takes and returns all parts, laid end to end along the dimension named above; an argument that names none is the same for every part. Nothing has to cross between parts.
Inputs may be any that keep to these rules, and one draw needn't show every extreme that they name: For each p, migrate[:, p] names every rank once, and the 8 pieces of one block go to every rank once. For each p, owners[:, p] names every rank once, and the 8 pieces of one block go to every rank once. `prompt_blocks`: the entries sum to 8.
All inputs are finite; a program needn't handle non-finite values.
Results may differ from a plain program's by a relative error of at most 0.012.
The roundings to bfloat16 on the way count: a program that leaves them out, or rounds other values in their place, can miss the bound.
Values may be sent and summed in bfloat16 or wider, within the bound.
A program may use at most 192 MiB of HBM per device.

v0:
```python
import math

import jax
import jax.numpy as jnp
from jax import lax
from jax.sharding import PartitionSpec as P

LAT = 512
ROPE = 64


def passed_along(block, axis, distance):
    devices = range(lax.axis_size(axis))
    route = [(i - distance, i) for i in devices if i - distance in devices]
    return lax.ppermute(block, axis, route)


def normalize(latent_raw, latent_gain):
    latent_part = latent_raw[:, :LAT]
    mean_square = jnp.mean(latent_part * latent_part, axis=-1, keepdims=True)
    normed = latent_part * lax.rsqrt(mean_square + 1e-06) * latent_gain.astype(jnp.float32)
    return jnp.concatenate([normed, latent_raw[:, LAT:]], axis=-1).astype(jnp.bfloat16)


def block_starts(prompt_blocks, rank_count):
    prompt_ends = jnp.cumsum(prompt_blocks)
    prompt_firsts = prompt_ends - prompt_blocks
    block_ids = jnp.arange(rank_count, dtype=jnp.int32)
    holder = jnp.sum((block_ids[:, None] >= prompt_ends[None, :]).astype(jnp.int32), axis=1)
    return jnp.take(prompt_firsts, holder)


def send_buffer(values, routes, my_rank, rank_count):
    piece_count = routes.shape[1]
    pieces = values.reshape(piece_count, values.shape[0] // piece_count, values.shape[1])
    own_routes = jnp.take(routes, my_rank, axis=0)
    one_hot = (own_routes[None, :] == jnp.arange(rank_count, dtype=jnp.int32)[:, None]).astype(
        jnp.bfloat16
    )
    return jnp.einsum("dp,prc->drc", one_hot, pieces, preferred_element_type=jnp.float32).astype(
        jnp.bfloat16
    )


def pick_slots(received, routes, my_rank):
    selector = (jnp.transpose(routes) == my_rank).astype(jnp.bfloat16)
    placed = jnp.einsum("pr,rqc->pqc", selector, received, preferred_element_type=jnp.float32)
    return placed.astype(jnp.bfloat16).reshape(-1, received.shape[2])


def body(hidden, w_down, latent_gain, queries, w_up_value, prompt_blocks, migrate, owners):
    tok_rows = hidden.shape[0]
    width = LAT + ROPE
    partial_latent = jnp.dot(hidden, w_down, preferred_element_type=jnp.float32)
    summed = lax.psum(partial_latent, "tensor")
    cache_rows = normalize(summed, latent_gain)
    my_rank = lax.axis_index("ranks")
    rank_count = lax.axis_size("ranks")
    span = rank_count // 2
    window = cache_rows[None]
    for level in range(span.bit_length() - 1):
        incoming = passed_along(window, "ranks", 2**level)
        window = jnp.concatenate([incoming, window], axis=0)
    starts = block_starts(prompt_blocks, rank_count)
    first_block = jnp.take(starts, my_rank)
    first_key = first_block * tok_rows
    lowest = jnp.maximum(first_block - my_rank + span - 1, 0)
    query_pos = my_rank * tok_rows + jnp.arange(tok_rows, dtype=jnp.int32)
    local_heads = queries.shape[1] // width
    group_size = 16
    group_count = local_heads // group_size
    grouped = jnp.transpose(queries.reshape(tok_rows, group_count, group_size, width), (1, 0, 2, 3))
    score_scale = 2.0 / math.sqrt(width)

    def attend(query_group):
        empty = jnp.full((group_size, tok_rows, span * tok_rows), -1e30, jnp.float32)

        def fill(block, buffer):
            keys = lax.dynamic_index_in_dim(window, block, 0, keepdims=False)
            scores = (
                jnp.einsum("thd,sd->hts", query_group, keys, preferred_element_type=jnp.float32)
                * score_scale
            )
            key_pos = (my_rank - (span - 1) + block) * tok_rows + jnp.arange(
                tok_rows, dtype=jnp.int32
            )
            allowed = (key_pos[None, :] >= first_key) & (key_pos[None, :] <= query_pos[:, None])
            scores = jnp.where(allowed[None], scores, jnp.float32(-1e30))
            return lax.dynamic_update_slice_in_dim(buffer, scores, block * tok_rows, 2)

        scores = lax.fori_loop(lowest, span, fill, empty)
        highest = jnp.max(scores, axis=-1, keepdims=True)
        expos = jnp.exp(scores - highest)
        probs = (expos / jnp.sum(expos, axis=-1, keepdims=True)).astype(jnp.bfloat16)

        def collect(block, running):
            weights = lax.dynamic_slice_in_dim(probs, block * tok_rows, tok_rows, 2)
            keys = lax.dynamic_index_in_dim(window, block, 0, keepdims=False)[:, :LAT]
            return running + jnp.einsum(
                "hts,sl->thl", weights, keys, preferred_element_type=jnp.float32
            )

        start_out = jnp.zeros((tok_rows, group_size, LAT), jnp.float32)
        return lax.fori_loop(lowest, span, collect, start_out).astype(jnp.bfloat16)

    grouped_out = lax.map(attend, grouped)
    latent_out = jnp.transpose(grouped_out, (1, 0, 2, 3)).reshape(tok_rows, local_heads, LAT)
    summed_values = jnp.einsum(
        "thl,hlv->thv",
        latent_out,
        lax.all_gather(w_up_value, "ranks", axis=1, tiled=True),
        preferred_element_type=jnp.float32,
    )
    head_out = summed_values.astype(jnp.bfloat16).reshape(
        tok_rows, local_heads * w_up_value.shape[2]
    )
    outgoing = send_buffer(head_out, migrate, my_rank, rank_count)
    arrived = lax.all_to_all(outgoing, "ranks", split_axis=0, concat_axis=0, tiled=True)
    served = pick_slots(arrived, migrate, my_rank)
    cache_out = send_buffer(cache_rows, owners, my_rank, rank_count)
    cache_in = lax.all_to_all(cache_out, "ranks", split_axis=0, concat_axis=0, tiled=True)
    cache_store = pick_slots(cache_in, owners, my_rank)
    return (served, cache_store)


def solution(mesh):
    placed = (
        P(("groups", "ranks"), "tensor"),
        P("tensor", None),
        P(),
        P(("groups", "ranks"), "tensor"),
        P("tensor", "ranks", None),
        P("groups"),
        P("groups", None),
        P("groups", None),
    )
    return jax.shard_map(
        body,
        mesh=mesh,
        in_specs=placed,
        out_specs=(P(("groups", "ranks"), "tensor"), P(("groups", "ranks"), None)),
        check_vma=False,
    )
```

profile of v0, /device:TPU:0, one launch (start us, length us, event | category | flops | bytes accessed | tf_op | source)
XLA Modules:
  0.0 257.2 jit_solution(17270459432907314874)
XLA Ops:
  8.0 0.0 all-reduce.2.cloned.1.call-start
  8.1 1.1 copy-done
  9.2 4.1 %fusion.36 = f32[128,576]{0,1:T(8,128)} fusion(bf16[128,3584]{1,0:T(8,128)(2,1)S(1)} %copy-done, bf16[3584,576]{0,1:T(8,128)(2,1)} %param.17), kind=kOutput, calls=%fused_computation.70 | convolution fusion | flops 528482304 | bytes 5341184 | tf_op jit(solution)/shard_map/dot_general | solution.py:54
  13.3 0.0 all-gather.2.cloned.1.call-start
  13.4 0.5 all-gather.2.cloned.1.call-update
  13.9 0.2 reduce-window.8
  14.1 0.1 convert_reduce_fusion
  14.2 0.6 gather_fusion
  14.8 19.6 %all-reduce.2.cloned.1.call-done = f32[128,576]{0,1:T(8,128)} async-done(((f32[128,576]{0,1:T(8,128)}), f32[128,576]{0,1:T(8,128)}) %all-reduce.2.cloned.1.call-update) | async-done | bytes 294928 | tf_op jit(solution)/shard_map/psum | solution.py:55
  34.5 1.0 multiply_reduce_fusion
  35.5 0.8 slice_bitcast_fusion.2
  36.3 1.1 fusion.42
  37.4 3.6 %collective-permute-start = (bf16[1,128,576]{1,2,0:T(8,128)(2,1)S(1)}, bf16[1,128,576]{1,2,0:T(8,128)(2,1)S(1)}, u32[]{:S(2)}, u32[]{:S(2)}) collective-permute-start(bf16[1,128,576]{1,2,0:T(8,128)(2,1)S(1)} %pad_maximum_fusion), channel_id=1, source_target_pairs={{0,2},{2,4},{4,6},{6,8},{8,10},{10,12},{12,14},{1,3},{3,5},{5,7},{... | collective-permute-start | bytes 442376 | tf_op jit(solution)/shard_map/ppermute | solution.py:15
  41.1 0.6 dynamic-slice.6
  42.3 6.7 %copy.45 = bf16[128,18432]{0,1:T(8,128)(2,1)} copy(bf16[128,18432]{1,0:T(8,128)(2,1)} %param.19) | data formatting | bytes 9437184 | tf_op args[3]
  49.0 1.3 fusion.32
  50.3 3.4 %collective-permute-start.1 = (bf16[2,128,576]{1,2,0:T(8,128)(2,1)S(1)}, bf16[2,128,576]{1,2,0:T(8,128)(2,1)S(1)}, u32[]{:S(2)}, u32[]{:S(2)}) collective-permute-start(bf16[2,128,576]{1,2,0:T(8,128)(2,1)S(1)} %maximum_maximum_fusion.1), channel_id=1, source_target_pairs={{0,4},{2,6},{4,8},{6,10},{8,12},{10,14},{1,5},{3,7},{5,9},{7,11},{... | collective-permute-start | bytes 884744 | tf_op jit(solution)/shard_map/ppermute | solution.py:15
  53.7 0.1 multiply_convert_fusion
  53.9 0.1 copy.53
  54.0 0.1 copy.55
  54.1 0.1 copy.54
  54.2 0.2 convolution_convert_fusion.4
  54.4 0.7 copy.57
  55.1 4.0 %all-to-all-start.1 = ((bf16[8,16,576]{2,1,0:T(8,128)(2,1)}), bf16[8,16,576]{2,1,0:T(8,128)(2,1)}, u32[]{:S(2)}, u32[]{:S(2)}) async-start(bf16[8,16,576]{2,1,0:T(8,128)(2,1)} %copy.57), calls=%async_computation.1 | async-start | bytes 327680 | tf_op jit(solution)/shard_map/all_to_all | solution.py:121
  59.1 7.9 %collective-permute-done.1 = bf16[2,128,576]{1,2,0:T(8,128)(2,1)S(1)} collective-permute-done((bf16[2,128,576]{1,2,0:T(8,128)(2,1)S(1)}, bf16[2,128,576]{1,2,0:T(8,128)(2,1)S(1)}, u32[]{:S(2)}, u32[]{:S(2)}) %collective-permute-start.1) | collective-permute-done | bytes 294944 | tf_op jit(solution)/shard_map/ppermute | solution.py:15
  67.0 0.9 maximum_maximum_fusion
  67.8 83.9 %while.69 = (s32[]{:T(128)}, bf16[2,128,16,512]{1,3,2,0:T(8,128)(2,1)}, bf16[2,128,16,576]{1,3,2,0:T(8,128)(2,1)}, s32[]{:T(128)}, s32[]{:T(128)}, /*index=5*/bf...) while((s32[]{:T(128)}, ...), condition=%wide.region_11.13_spmd.clone, body=%wide.region_4.12_spmd.clone.sunk | while | flops 578323456 | bytes 51220020 | solution.py:106
  67.8 1.8 dynamic-slice_bitcast_fusion.4
  69.7 2.4 broadcast.188
  72.1 2.7 %while.70 = (s32[]{:T(128)}, f32[16,128,512]{1,2,0:T(8,128)}, s32[]{:T(128)}, s32[]{:T(128)}, s32[128]{0:T(128)S(1)}, /*index=5*/bf16[4,128,576]{1,2,0:T(8,128)(...) while((s32[]{:T(128)}, f32[16,128,512]{1,2,0:T(8,128)}, ...), condition=%wide.region_6.7_spmd, body=%wide.region_5.6_spmd.sunk | while | flops 302547328 | bytes 3590129 | solution.py:91
  72.1 0.1 compare_and_fusion.2
  72.2 2.6 fusion.49
  74.7 5.4 %copy.74 = f32[16,128,512]{2,1,0:T(8,128)} copy(f32[16,128,512]{1,2,0:T(8,128)} %get-tuple-element.497) | data formatting | bytes 8388608 | tf_op jit(solution)/shard_map/while/body/eval_jaxpr/while | solution.py:91
  80.1 2.5 reduce_max.16
  82.6 15.2 %divide_convert_fusion.2 = bf16[16,128,512]{2,1,0:T(8,128)(2,1)S(1)} fusion(f32[16,128,512]{2,1,0:T(8,128)} %copy.74, f32[16,128]{1,0:T(8,128)S(1)} %reduce_max.16), kind=kOutput, calls=%fused_computation.18.clone.1 | output fusion | flops 4196863 | bytes 6299648 | tf_op jit(solution)/shard_map/while/body/eval_jaxpr/div | solution.py:94
  97.8 2.4 broadcast.187
  100.1 5.8 %while.71 = (s32[]{:T(128)}, f32[128,16,512]{0,2,1:T(8,128)}, bf16[4,128,576]{1,2,0:T(8,128)(2,1)}, bf16[16,128,512]{2,1,0:T(8,128)(2,1)S(1)}, s32[]{:T(128)}, /*index=5*/s32[]{:T(128)}, s32[]{:T(128)}, s32[]{:T(128)}, s32[]{:T(128)}) while((s32[]{:T(128)}, f32[128,16,512]{0,2,1:T(8,128)}, bf16[4,128,576]{1,2,0:T(8,128)(2,1)}, ...), condition=%wide.region_10.11_spmd, body=%wide.region_9.10_spmd.sunk | while | flops 269484032 | bytes 9339061 | solution.py:104
  100.1 0.9 dynamic-slice_bitcast_fusion.5
  101.1 4.9 %bitcast_add_fusion.2 = f32[128,16,512]{0,2,1:T(8,128)} fusion(f32[128,16,512]{0,2,1:T(8,128)} %get-tuple-element.556, bf16[16,128,512]{2,1,0:T(8,128)(2,1)S(1)} %get-tuple-element.567, s32[]{:T(128)S(6)} %select_n.96, bf16[128,576]{0,1:T(8,128)(2,1)S(1)} %dynamic-slice_bitcast_fusion.5), kind=kOutput, calls=%fused_computation.12.clone.1 | convolution fusion | flops 269484032 | bytes 9043972 | tf_op jit(solution)/shard_map/while/body/eval_jaxpr/while/body/hts,sl->thl/dot_general | solution.py:99
  105.9 3.9 %bitcast_dynamic-update-slice_fusion.2 = bf16[2,128,16,512]{1,3,2,0:T(8,128)(2,1)} fusion(bf16[2,128,16,512]{1,3,2,0:T(8,128)(2,1)} %get-tuple-element.596, s32[]{:T(128)} %get-tuple-element.595, f32[128,16,512]{0,2,1:T(8,128)} %get-tuple-element.498), kind=kLoop, calls=%fused_computation.22.clone.1 | loop fusion | flops 1048576 | bytes 6291968 | tf_op jit(solution)/shard_map/while/body/jit(dynamic_update_index_in_dim)/dynamic_update_slice | solution.py:106
  109.9 1.8 dynamic-slice_bitcast_fusion.4
  111.7 2.4 broadcast.188
  114.1 2.7 %while.70 = (s32[]{:T(128)}, f32[16,128,512]{1,2,0:T(8,128)}, s32[]{:T(128)}, s32[]{:T(128)}, s32[128]{0:T(128)S(1)}, /*index=5*/bf16[4,128,576]{1,2,0:T(8,128)(...) while((s32[]{:T(128)}, f32[16,128,512]{1,2,0:T(8,128)}, ...), condition=%wide.region_6.7_spmd, body=%wide.region_5.6_spmd.sunk | while | flops 302547328 | bytes 3590129 | solution.py:91
  114.1 0.1 compare_and_fusion.2
  114.2 2.6 fusion.49
  116.8 5.3 %copy.74 = f32[16,128,512]{2,1,0:T(8,128)} copy(f32[16,128,512]{1,2,0:T(8,128)} %get-tuple-element.497) | data formatting | bytes 8388608 | tf_op jit(solution)/shard_map/while/body/eval_jaxpr/while | solution.py:91
  122.1 2.4 reduce_max.16
  124.5 15.1 %divide_convert_fusion.2 = bf16[16,128,512]{2,1,0:T(8,128)(2,1)S(1)} fusion(f32[16,128,512]{2,1,0:T(8,128)} %copy.74, f32[16,128]{1,0:T(8,128)S(1)} %reduce_max.16), kind=kOutput, calls=%fused_computation.18.clone.1 | output fusion | flops 4196863 | bytes 6299648 | tf_op jit(solution)/shard_map/while/body/eval_jaxpr/div | solution.py:94
  139.6 2.4 broadcast.187
  142.0 5.8 %while.71 = (s32[]{:T(128)}, f32[128,16,512]{0,2,1:T(8,128)}, bf16[4,128,576]{1,2,0:T(8,128)(2,1)}, bf16[16,128,512]{2,1,0:T(8,128)(2,1)S(1)}, s32[]{:T(128)}, /*index=5*/s32[]{:T(128)}, s32[]{:T(128)}, s32[]{:T(128)}, s32[]{:T(128)}) while((s32[]{:T(128)}, f32[128,16,512]{0,2,1:T(8,128)}, bf16[4,128,576]{1,2,0:T(8,128)(2,1)}, ...), condition=%wide.region_10.11_spmd, body=%wide.region_9.10_spmd.sunk | while | flops 269484032 | bytes 9339061 | solution.py:104
  142.0 0.9 dynamic-slice_bitcast_fusion.5
  142.9 4.9 %bitcast_add_fusion.2 = f32[128,16,512]{0,2,1:T(8,128)} fusion(f32[128,16,512]{0,2,1:T(8,128)} %get-tuple-element.556, bf16[16,128,512]{2,1,0:T(8,128)(2,1)S(1)} %get-tuple-element.567, s32[]{:T(128)S(6)} %select_n.96, bf16[128,576]{0,1:T(8,128)(2,1)S(1)} %dynamic-slice_bitcast_fusion.5), kind=kOutput, calls=%fused_computation.12.clone.1 | convolution fusion | flops 269484032 | bytes 9043972 | tf_op jit(solution)/shard_map/while/body/eval_jaxpr/while/body/hts,sl->thl/dot_general | solution.py:99
  147.8 3.9 %bitcast_dynamic-update-slice_fusion.2 = bf16[2,128,16,512]{1,3,2,0:T(8,128)(2,1)} fusion(bf16[2,128,16,512]{1,3,2,0:T(8,128)(2,1)} %get-tuple-element.596, s32[]{:T(128)} %get-tuple-element.595, f32[128,16,512]{0,2,1:T(8,128)} %get-tuple-element.498), kind=kLoop, calls=%fused_computation.22.clone.1 | loop fusion | flops 1048576 | bytes 6291968 | tf_op jit(solution)/shard_map/while/body/jit(dynamic_update_index_in_dim)/dynamic_update_slice | solution.py:106
  151.7 4.8 %fusion.13 = bf16[128,32,128]{2,0,1:T(8,128)(2,1)S(1)} fusion(bf16[128,32,512]{0,2,1:T(8,128)(2,1)} %bitcast.84, bf16[32,512,128]{2,1,0:T(8,128)(2,1)} %all-gather.2.cloned.1.call-done), kind=kOutput, calls=%fused_computation.28 | convolution fusion | flops 537395200 | bytes 9437184 | tf_op jit(solution)/shard_map/thl,hlv->thv/dot_general | solution.py:108
  156.5 0.7 copy.47
  157.2 0.5 reshape_reshape.3
  157.8 1.3 convolution_convert_fusion.1
  159.0 1.6 copy.49
  160.6 61.0 %all-to-all-start = ((bf16[8,16,4096]{2,1,0:T(8,128)(2,1)}), bf16[8,16,4096]{2,1,0:T(8,128)(2,1)S(1)}, u32[]{:S(2)}, u32[]{:S(2)}) async-start(bf16[8,16,4096]{2,1,0:T(8,128)(2,1)} %copy.49), calls=%async_computation | async-start | bytes 2097152 | tf_op jit(solution)/shard_map/all_to_all | solution.py:118
  221.5 1.2 convolution_convert_fusion.3
  222.7 0.8 copy.61
  223.5 23.5 %all-to-all-done = bf16[8,16,4096]{2,1,0:T(8,128)(2,1)S(1)} async-done(((bf16[8,16,4096]{2,1,0:T(8,128)(2,1)}), bf16[8,16,4096]{2,1,0:T(8,128)(2,1)S(1)}, u32[]{:S(2)}, u32[]{:S(2)}) %all-to-all-start) | async-done | bytes 1048608 | tf_op jit(solution)/shard_map/all_to_all | solution.py:118
  247.0 1.2 convolution_convert_fusion
  248.2 1.6 copy.52
  (35 shorter events, 0.2 us)
Async XLA Ops:
  8.0 1.2 copy-start
  8.0 5.9 %copy-start.6 = (s32[4]{0:T(128)S(1)}, s32[4]{0:T(128)}, u32[]{:S(2)}) copy-start(s32[4]{0:T(128)} %param.21) | copy-start | bytes 52
  8.0 6.2 %copy-start.5 = (bf16[512]{0:T(512)(128)(2,1)S(1)}, bf16[512]{0:T(512)(128)(2,1)}, u32[]{:S(2)}) copy-start(bf16[512]{0:T(512)(128)(2,1)} %param.18) | copy-start | bytes 3076
  8.0 26.5 %all-reduce.2.cloned.1.call-start = ((), (), s32[]{:S(2)}) async-start(), calls=%async_computation.2 | async-start | bytes 589824 | tf_op jit(solution)/shard_map/psum | solution.py:55
  13.3 138.4 %all-gather.2.cloned.1.call-start = ((), (), s32[]{:S(2)}) async-start(), calls=%async_computation.3 | async-start | bytes 4718592 | tf_op jit(solution)/shard_map/all_gather | solution.py:111
  37.4 12.9 %collective-permute-start = (bf16[1,128,576]{1,2,0:T(8,128)(2,1)S(1)}, bf16[1,128,576]{1,2,0:T(8,128)(2,1)S(1)}, u32[]{:S(2)}, u32[]{:S(2)}) collective-permute-start(bf16[1,128,576]{1,2,0:T(8,128)(2,1)S(1)} %pad_maximum_fusion), channel_id=1, source_target_pairs={{0,2},{2,4},{4,6},{6,8},{8,10},{10,12},{12,14},{1,3},{3,5},{5,7},{... | collective-permute-start | bytes 442376 | tf_op jit(solution)/shard_map/ppermute | solution.py:15
  42.3 11.4 %copy-start.1 = (f32[128,576]{0,1:T(8,128)S(1)}, f32[128,576]{0,1:T(8,128)}, u32[]{:S(2)}) copy-start(f32[128,576]{0,1:T(8,128)} %all-reduce.2.cloned.1.call-done) | copy-start | bytes 884740
  50.3 16.7 %collective-permute-start.1 = (bf16[2,128,576]{1,2,0:T(8,128)(2,1)S(1)}, bf16[2,128,576]{1,2,0:T(8,128)(2,1)S(1)}, u32[]{:S(2)}, u32[]{:S(2)}) collective-permute-start(bf16[2,128,576]{1,2,0:T(8,128)(2,1)S(1)} %maximum_maximum_fusion.1), channel_id=1, source_target_pairs={{0,4},{2,6},{4,8},{6,10},{8,12},{10,14},{1,5},{3,7},{5,9},{7,11},{... | collective-permute-start | bytes 884744 | tf_op jit(solution)/shard_map/ppermute | solution.py:15
  55.1 105.5 %all-to-all-start.1 = ((bf16[8,16,576]{2,1,0:T(8,128)(2,1)}), bf16[8,16,576]{2,1,0:T(8,128)(2,1)}, u32[]{:S(2)}, u32[]{:S(2)}) async-start(bf16[8,16,576]{2,1,0:T(8,128)(2,1)} %copy.57), calls=%async_computation.1 | async-start | bytes 327680 | tf_op jit(solution)/shard_map/all_to_all | solution.py:121
  156.5 1.2 copy-start.4
  157.2 64.3 %copy-start.3 = (s32[8,8]{1,0:T(8,128)S(1)}, s32[8,8]{1,0:T(8,128)}, u32[]{:S(2)}) copy-start(s32[8,8]{1,0:T(8,128)} %param.23) | copy-start | bytes 772
  157.2 89.8 %copy-start.2 = (s32[8,8]{1,0:T(8,128)S(1)}, s32[8,8]{1,0:T(8,128)}, u32[]{:S(2)}) copy-start(s32[8,8]{1,0:T(8,128)} %param.22) | copy-start | bytes 772
  160.6 86.4 %all-to-all-start = ((bf16[8,16,4096]{2,1,0:T(8,128)(2,1)}), bf16[8,16,4096]{2,1,0:T(8,128)(2,1)S(1)}, u32[]{:S(2)}, u32[]{:S(2)}) async-start(bf16[8,16,4096]{2,1,0:T(8,128)(2,1)} %copy.49), calls=%async_computation | async-start | bytes 2097152 | tf_op jit(solution)/shard_map/all_to_all | solution.py:118
Sparse Core Ops, SparseCore 0:
  13.4 21.0 all-reduce.1
Sparse Core Ops, SparseCore 1:
  16.0 80.8 all-gather.1
where the time goes:
time: 257 us
  starting transfers between devices  72.1 us (28%)
  waiting for transfers between devices  51.5 us (20%)
  other arithmetic  47.9 us (19%)
  local copies, waits for them, and re-layouts  41.6 us (16%)
  matrix products  27.6 us (11%)
  between operations  16.4 us (6%)
    all_to_all x1, starting transfers between devices, body(): lax.all_to_all(outgoing, 'ranks', split_axis=0, concat_axis=0, tiled=True)  61 us
    div x2, other arithmetic, attend(): expos / jnp.sum(expos, axis=-1, keepdims=True)  30.3 us
    all_to_all x1, waiting for transfers between devices, body(): lax.all_to_all(outgoing, 'ranks', split_axis=0, concat_axis=0, tiled=True)  23.5 us
    psum x1, waiting for transfers between devices, body(): summed = lax.psum(partial_latent, 'tensor')  19.6 us
    while x2, local copies, waits for them, and re-layouts, attend(): scores = lax.fori_loop(lowest, span, fill, empty)  10.7 us
    dot_general x2, matrix products, collect(): jnp.einsum('hts,sl->thl', weights, keys, preferred_element_type=jnp.float32)  9.71 us
    another operation x6, local copies, waits for them, and re-layouts  9.68 us
    unnamed x16, local copies, waits for them, and re-layouts  8.62 us
  transfers between devices with their start and end apart: 6, of which 3 were waited for; matrix products, arithmetic and copies ran while one was open for 42% of the time, Pallas kernels for 0%

commit v1 on v0

--- a/solution.py
+++ b/solution.py
@@ -1,8 +1,11 @@
+import functools
 import math
 
 import jax
 import jax.numpy as jnp
 from jax import lax
+from jax.experimental import pallas as pl
+from jax.experimental.pallas import tpu as pltpu
 from jax.sharding import PartitionSpec as P
 
 LAT = 512
@@ -123,7 +126,459 @@
     return (served, cache_store)
 
 
+PIECE = 16
+WIDE = LAT + 2 * ROPE
+BLOCKS = 4
+GROUPS = 4
+MESH = pl.DeviceIdType.MESH
+
+
+def remote(src, dst, send_sem, recv_sem, where):
+    return pltpu.make_async_remote_copy(
+        src_ref=src,
+        dst_ref=dst,
+        send_sem=send_sem,
+        recv_sem=recv_sem,
+        device_id=where,
+        device_id_type=MESH,
+    )
+
+
+def by_piece(index, values):
+    out = jnp.zeros_like(index)
+    for p, value in enumerate(values):
+        out = jnp.where((index // PIECE) == p, value, out)
+    return out
+
+
+def send_matrix(routes, me, n):
+    rows = lax.broadcasted_iota(jnp.int32, (n * PIECE, n * PIECE), 0)
+    cols = lax.broadcasted_iota(jnp.int32, (n * PIECE, n * PIECE), 1)
+    target = by_piece(cols, [routes[me, p] for p in range(n)])
+    hit = ((rows // PIECE) == target) & ((rows % PIECE) == (cols % PIECE))
+    return jnp.where(hit, 1.0, 0.0).astype(jnp.bfloat16)
+
+
+def take_matrix(routes, me, n):
+    rows = lax.broadcasted_iota(jnp.int32, (n * PIECE, n * PIECE), 0)
+    cols = lax.broadcasted_iota(jnp.int32, (n * PIECE, n * PIECE), 1)
+    origins = []
+    for p in range(n):
+        origin = jnp.int32(0)
+        for r in range(n):
+            origin = origin + jnp.where(routes[r, p] == me, r, 0)
+        origins.append(origin)
+    source = by_piece(rows, origins)
+    hit = ((cols // PIECE) == source) & ((rows % PIECE) == (cols % PIECE))
+    return jnp.where(hit, 1.0, 0.0).astype(jnp.bfloat16)
+
+
+def kernel(
+    n, hidden, w_down, gain, queries, w_up, prompt_blocks, migrate, owners,
+    served, store,
+    hid, wd, qbuf, wall, part, part_in, key0, key1, latent, bias, out_mat, in_mat,
+    send, recv, csend, crecv,
+    hid_sem, wd_sem, q_sem, own_sem, part_sem, key_send, key_recv,
+    y_send, up_send, down_send, x_send, w_recv, send_sem, recv_sem, c_send, c_recv,
+):
+    me = lax.axis_index("ranks")
+    x = lax.axis_index("groups")
+    core = lax.axis_index("tensor")
+    z, y = me // 2, me % 2
+    levels = n // 2
+    tok = hid.shape[0]
+    heads = w_up.shape[0]
+    half = heads // 2
+    pairs = heads // 2
+    twin = 2 * z + (1 - y)
+    other_x = {"groups": 1 - x}
+
+    chunks = wd_sem.shape[0]
+    rows = wd.shape[0] // chunks
+    hid_copy = pltpu.make_async_copy(hidden, hid, hid_sem)
+    hid_copy.start()
+    wd_copies = []
+    for c in range(chunks):
+        cut = pl.ds(c * rows, rows)
+        wd_copies.append(pltpu.make_async_copy(w_down.at[cut], wd.at[cut], wd_sem.at[c]))
+        wd_copies[-1].start()
+
+    barrier = pltpu.get_barrier_semaphore()
+    for k in range(1, n):
+        pl.semaphore_signal(barrier, 1, device_id={"ranks": (me + k) % n}, device_id_type=MESH)
+    pl.semaphore_signal(barrier, 1, device_id={"tensor": 1 - core}, device_id_type=MESH)
+    pl.semaphore_signal(barrier, 1, device_id=other_x, device_id_type=MESH)
+    pl.semaphore_wait(barrier, n + 1)
+
+    def hcut(h):
+        return pl.ds(h * half, half)
+
+    def slot(r, h):
+        return wall.at[r, hcut(h)]
+
+    def hop(sems, src, r, h, where):
+        return remote(src, slot(r, h), sems.at[r, h], w_recv.at[r, h], where)
+
+    y_first = hop(y_send, w_up.at[hcut(x)], me, x, {"ranks": twin})
+    y_last = hop(y_send, w_up.at[hcut(1 - x)], me, 1 - x, {"ranks": twin})
+    own_copy = pltpu.make_async_copy(w_up, wall.at[me], own_sem)
+
+    def up_hop(r, src):
+        return hop(up_send, src, r, x, {"ranks": jnp.minimum(me + 2, n - 2 + y)})
+
+    def down_hop(r, src):
+        return hop(down_send, src, r, x, {"ranks": jnp.maximum(me - 2, y)})
+
+    def x_hop(r):
+        return hop(x_send, slot(r, x), r, x, other_x)
+
+    def arrived(r, h):
+        remote(slot(r, h), slot(r, h), x_send.at[r, h], w_recv.at[r, h], other_x).wait_recv()
+
+    y_first.start()
+
+    @pl.when(z < levels - 1)
+    def _():
+        up_hop(me, w_up.at[hcut(x)]).start()
+
+    @pl.when(z > 0)
+    def _():
+        down_hop(me, w_up.at[hcut(x)]).start()
+
+    q_copies = []
+    for parity in range(2):
+        for i in range(pairs):
+            q_copies.append(
+                pltpu.make_async_copy(
+                    queries.at[:, pl.ds(i * 2 * (LAT + ROPE) + parity * LAT, WIDE)],
+                    qbuf.at[parity, i],
+                    q_sem.at[parity, i],
+                )
+            )
+            q_copies[-1].start()
+    own_copy.start()
+    y_last.start()
+
+    hid_copy.wait()
+    for c in range(chunks):
+        wd_copies[c].wait()
+        term = jnp.dot(
+            hid[:, c * rows : (c + 1) * rows],
+            wd[c * rows : (c + 1) * rows, :],
+            preferred_element_type=jnp.float32,
+        )
+        part[...] = term if c == 0 else part[...] + term
+    part_copy = remote(part, part_in, part_sem.at[0], part_sem.at[1], {"tensor": 1 - core})
+    part_copy.start()
+
+    out_mat[0] = send_matrix(migrate, me, n)
+    out_mat[1] = send_matrix(owners, me, n)
+    in_mat[0] = take_matrix(migrate, me, n)
+    in_mat[1] = take_matrix(owners, me, n)
+    first = jnp.int32(0)
+    end = jnp.int32(0)
+    for i in range(prompt_blocks.shape[0]):
+        end = end + prompt_blocks[i]
+        first = jnp.where(me >= end, end, first)
+    query_pos = me * tok + lax.broadcasted_iota(jnp.int32, (tok, BLOCKS * tok), 0)
+    key_pos = (me - (BLOCKS - 1)) * tok + lax.broadcasted_iota(jnp.int32, (tok, BLOCKS * tok), 1)
+    allowed = (key_pos >= first * tok) & (key_pos <= query_pos)
+    bias[...] = jnp.where(allowed, 0.0, -1e30)
+
+    part_copy.wait()
+    raw = part[...] + part_in[...]
+    lead = raw[:, :LAT]
+    mean_square = jnp.mean(lead * lead, axis=-1, keepdims=True)
+    normed = lead * lax.rsqrt(mean_square + 1e-06) * gain[...].astype(jnp.float32)
+    rope = raw[:, LAT:]
+    blank = jnp.zeros((tok, ROPE), jnp.float32)
+    key0[BLOCKS - 1] = jnp.concatenate([normed, rope, blank], axis=-1).astype(jnp.bfloat16)
+
+    def key_copy(d, r):
+        return remote(
+            key0.at[BLOCKS - 1], key0.at[BLOCKS - 1 - d], key_send.at[d], key_recv.at[d], {"ranks": r}
+        )
+
+    for d in range(1, BLOCKS):
+        @pl.when(me + d < n)
+        def _():
+            key_copy(d, (me + d) % n).start()
+
+    arrived(twin, x)
+
+    @pl.when(z < levels - 1)
+    def _():
+        up_hop(twin, slot(twin, x)).start()
+
+    @pl.when(z > 0)
+    def _():
+        down_hop(twin, slot(twin, x)).start()
+
+    csend[...] = (
+        jnp.dot(out_mat[1], key0[BLOCKS - 1], preferred_element_type=jnp.float32)
+        .astype(jnp.bfloat16)
+        .reshape(n, PIECE, WIDE)
+    )
+    crecv[me] = csend[me]
+
+    def c_copy(k):
+        to = (me + k) % n
+        return remote(csend.at[to], crecv.at[me], c_send.at[to], c_recv.at[me], {"ranks": to})
+
+    for k in range(1, n):
+        c_copy(k).start()
+
+    for d in range(1, BLOCKS):
+        @pl.when(me >= d)
+        def _():
+            key_copy(d, (me + d) % n).wait_recv()
+
+        @pl.when(me < d)
+        def _():
+            key0[BLOCKS - 1 - d] = jnp.zeros((tok, WIDE), jnp.bfloat16)
+
+    for b in range(BLOCKS):
+        key1[b] = jnp.concatenate(
+            [jnp.zeros((tok, ROPE), jnp.bfloat16), key0[b][:, : LAT + ROPE]], axis=-1
+        )
+
+    def relay(d, same):
+        def row(level):
+            return 2 * level + (y if same else 1 - y)
+
+        @pl.when(z >= d)
+        def _():
+            r = row(jnp.maximum(z - d, 0))
+            arrived(r, x)
+            if d < levels - 1:
+                @pl.when(z < levels - 1)
+                def _():
+                    up_hop(r, slot(r, x)).start()
+
+            x_hop(r).start()
+
+        @pl.when(z + d < levels)
+        def _():
+            r = row(jnp.minimum(z + d, levels - 1))
+            arrived(r, x)
+            if d < levels - 1:
+                @pl.when(z > 0)
+                def _():
+                    down_hop(r, slot(r, x)).start()
+
+            x_hop(r).start()
+
+    factor = 2.0 / math.sqrt(LAT + ROPE) * math.log2(math.e)
+    step = 4
+
+    def attend(parity, keys, g):
+        at = pl.ds(g * step, step)
+        q = qbuf[parity, at].reshape(step * tok, WIDE)
+        s = lax.dot_general(
+            q,
+            keys[...].reshape(BLOCKS * tok, WIDE),
+            (((1,), (1,)), ((), ())),
+            preferred_element_type=jnp.float32,
+        )
+        s = s.reshape(step, tok, BLOCKS * tok) + bias[...][None]
+        top = jnp.max(s, axis=-1, keepdims=True)
+        e = jnp.exp2((s - top) * factor)
+        p = (e * (1.0 / jnp.sum(e, axis=-1, keepdims=True))).astype(jnp.bfloat16)
+        out = jnp.dot(
+            p.reshape(step * tok, BLOCKS * tok),
+            key0[:, :, :LAT].reshape(BLOCKS * tok, LAT),
+            preferred_element_type=jnp.float32,
+        )
+        latent[parity, at] = out.astype(jnp.bfloat16).reshape(step, tok, LAT)
+
+    events = [(d, same) for d in range(1, levels) for same in (True, False)]
+    plan = [events[:1], events[1:2], events[2:3], events[3:4], events[4:]]
+    for copy in q_copies:
+        copy.wait()
+    spots = iter(plan)
+    for parity, keys in ((0, key0), (1, key1)):
+        for lower in (0, 2):
+            for event in next(spots):
+                relay(*event)
+
+            def some(g, carry, parity=parity, keys=keys):
+                attend(parity, keys, g)
+                return carry
+
+            lax.fori_loop(lower, lower + 2, some, 0)
+    for event in next(spots):
+        relay(*event)
+
+    group = heads // GROUPS
+    wide = group * w_up.shape[2]
+    vdim = w_up.shape[2]
+
+    def gcols(g):
+        return pl.ds(pl.multiple_of(g * wide, wide), wide)
+
+    def piece_copy(g, k):
+        to = (me + k) % n
+        return remote(
+            send.at[to, :, gcols(g)],
+            recv.at[me, :, gcols(g)],
+            send_sem.at[g, to],
+            recv_sem.at[g, me],
+            {"ranks": to},
+        )
+
+    def project(g):
+        def one(i, carry):
+            for parity in range(2):
+                h = g * group + 2 * i + parity
+                w = wall[:, h].reshape(LAT, vdim)
+                out = jnp.dot(
+                    latent[parity, g * (group // 2) + i], w, preferred_element_type=jnp.float32
+                ).astype(jnp.bfloat16)
+                moved = jnp.dot(out_mat[0], out, preferred_element_type=jnp.float32)
+                cols = pl.ds(pl.multiple_of(h * vdim, vdim), vdim)
+                send[:, :, cols] = moved.astype(jnp.bfloat16).reshape(n, PIECE, vdim)
+            return carry
+
+        lax.fori_loop(0, group // 2, one, 0)
+        for k in range(1, n):
+            piece_copy(g, k).start()
+        recv[me, :, gcols(g)] = send[me, :, gcols(g)]
+
+    own_copy.wait()
+    for i in range(GROUPS // 2):
+        project(x * (GROUPS // 2) + i)
+    arrived(twin, 1 - x)
+    for d in range(1, levels):
+        for same in (True, False):
+            def row(level):
+                return 2 * level + (y if same else 1 - y)
+
+            @pl.when(z >= d)
+            def _():
+                arrived(row(jnp.maximum(z - d, 0)), 1 - x)
+
+            @pl.when(z + d < levels)
+            def _():
+                arrived(row(jnp.minimum(z + d, levels - 1)), 1 - x)
+
+    for i in range(GROUPS // 2):
+        project((1 - x) * (GROUPS // 2) + i)
+
+    for k in range(1, n):
+        r = (me + k) % n
+        remote(csend.at[r], crecv.at[r], c_send.at[r], c_recv.at[r], {"ranks": r}).wait_recv()
+    kept = jnp.dot(
+        in_mat[1], crecv[...].reshape(n * PIECE, WIDE), preferred_element_type=jnp.float32
+    )
+    store[...] = kept[:, : LAT + ROPE].astype(jnp.bfloat16)
+    for i in range(GROUPS):
+        g = (x * (GROUPS // 2) + i) % GROUPS
+        for k in range(1, n):
+            r = (me + k) % n
+            remote(
+                send.at[r, :, gcols(g)],
+                recv.at[r, :, gcols(g)],
+                send_sem.at[g, r],
+                recv_sem.at[g, r],
+                {"ranks": r},
+            ).wait_recv()
+        served[:, gcols(g)] = jnp.dot(
+            in_mat[0],
+            recv[:, :, gcols(g)].reshape(n * PIECE, wide),
+            preferred_element_type=jnp.float32,
+        ).astype(jnp.bfloat16)
+
+    y_first.wait_send()
+    y_last.wait_send()
+    for d in range(1, BLOCKS):
+        @pl.when(me + d < n)
+        def _():
+            key_copy(d, (me + d) % n).wait_send()
+
+    for k in range(1, n):
+        c_copy(k).wait_send()
+        for g in range(GROUPS):
+            piece_copy(g, k).wait_send()
+    for level_at in range(levels):
+        for same in (True, False):
+            r = 2 * level_at + (y if same else 1 - y)
+
+            @pl.when((z >= level_at) & (z < levels - 1))
+            def _():
+                up_hop(r, slot(r, x)).wait_send()
+
+            @pl.when((z <= level_at) & (z > 0))
+            def _():
+                down_hop(r, slot(r, x)).wait_send()
+
+            @pl.when(z != level_at)
+            def _():
+                x_hop(r).wait_send()
+
+
+def fused(hidden, w_down, latent_gain, queries, w_up_value, prompt_blocks, migrate, owners):
+    n = lax.axis_size("ranks")
+    tok, depth = hidden.shape
+    heads, _, vdim = w_up_value.shape
+    any_space = pl.BlockSpec(memory_space=pl.ANY)
+    vmem = pl.BlockSpec(memory_space=pltpu.VMEM)
+    smem = pl.BlockSpec(memory_space=pltpu.SMEM)
+    bf16 = jnp.bfloat16
+    dma = pltpu.SemaphoreType.DMA
+    return pl.pallas_call(
+        functools.partial(kernel, n),
+        out_shape=(
+            jax.ShapeDtypeStruct((tok, heads * vdim), bf16),
+            jax.ShapeDtypeStruct((tok, LAT + ROPE), bf16),
+        ),
+        in_specs=[any_space, any_space, vmem, any_space, any_space, smem, smem, smem],
+        out_specs=(vmem, vmem),
+        scratch_shapes=[
+            pltpu.VMEM((tok, depth), bf16),
+            pltpu.VMEM((depth, LAT + ROPE), bf16),
+            pltpu.VMEM((2, heads // 2, tok, WIDE), bf16),
+            pltpu.VMEM((n, heads, w_up_value.shape[1], vdim), bf16),
+            pltpu.VMEM((tok, LAT + ROPE), jnp.float32),
+            pltpu.VMEM((tok, LAT + ROPE), jnp.float32),
+            pltpu.VMEM((BLOCKS, tok, WIDE), bf16),
+            pltpu.VMEM((BLOCKS, tok, WIDE), bf16),
+            pltpu.VMEM((2, heads // 2, tok, LAT), bf16),
+            pltpu.VMEM((tok, BLOCKS * tok), jnp.float32),
+            pltpu.VMEM((2, tok, tok), bf16),
+            pltpu.VMEM((2, tok, tok), bf16),
+            pltpu.VMEM((n, PIECE, heads * vdim), bf16),
+            pltpu.VMEM((n, PIECE, heads * vdim), bf16),
+            pltpu.VMEM((n, PIECE, WIDE), bf16),
+            pltpu.VMEM((n, PIECE, WIDE), bf16),
+            dma(()),
+            dma((4,)),
+            dma((2, heads // 2)),
+            dma(()),
+            dma((2,)),
+            dma((BLOCKS,)),
+            dma((BLOCKS,)),
+            dma((n, 2)),
+            dma((n, 2)),
+            dma((n, 2)),
+            dma((n, 2)),
+            dma((n, 2)),
+            dma((GROUPS, n)),
+            dma((GROUPS, n)),
+            dma((n,)),
+            dma((n,)),
+        ],
+        compiler_params=pltpu.CompilerParams(
+            collective_id=0, has_side_effects=True, vmem_limit_bytes=52 * 1024 * 1024
+        ),
+    )(
+        hidden, w_down, latent_gain.reshape(1, LAT), queries, w_up_value,
+        prompt_blocks, migrate, owners,
+    )
+
+
 def solution(mesh):
+    sizes = dict(mesh.shape)
+    small = sizes["ranks"] == 8 and sizes["groups"] == 2 and sizes["tensor"] == 2
     placed = (
         P(("groups", "ranks"), "tensor"),
         P("tensor", None),
@@ -135,7 +590,7 @@
         P("groups", None),
     )
     return jax.shard_map(
-        body,
+        fused if small else body,
         mesh=mesh,
         in_specs=placed,
         out_specs=(P(("groups", "ranks"), "tensor"), P(("groups", "ranks"), None)),

time: 257 us -> 91.9 us (0.36)
  Pallas kernels: 0 us -> 80.5 us
  starting transfers between devices: 72.1 us -> 0 us
  waiting for transfers between devices: 51.5 us -> 0 us
  other arithmetic: 47.9 us -> 0 us
  local copies, waits for them, and re-layouts: 41.6 us -> 10.4 us
  matrix products: 27.6 us -> 0 us
  between operations: 16.4 us -> 0.7 us
    pallas_call x0 -> x1, Pallas kernels: none -> 80.5 us  [fused(): pl.pallas_call(functools.partial(kernel, n), out_shape=(jax.ShapeDtypeStr...]
    all_to_all x2 -> x0, starting transfers between devices: 65 us -> none  [the longest x1 61 us: body(): lax.all_to_all(outgoing, 'ranks', split_axis=0, concat_axis=0, tiled=True)]
    div x2 -> x0, other arithmetic: 30.3 us -> none  [attend(): expos / jnp.sum(expos, axis=-1, keepdims=True)]
    dot_general x10 -> x0, matrix products: 27.6 us -> none  [the longest x2 9.71 us: collect(): jnp.einsum('hts,sl->thl', weights, keys, preferred_element_type=jnp.float32)]
    all_to_all x2 -> x0, waiting for transfers between devices: 23.5 us -> none  [the longest x1 23.5 us: body(): lax.all_to_all(outgoing, 'ranks', split_axis=0, concat_axis=0, tiled=True)]
    psum x1 -> x0, waiting for transfers between devices: 19.6 us -> none  [body(): summed = lax.psum(partial_latent, 'tensor')]
    another operation x8 -> x0, local copies, waits for them, and re-layouts: 10.8 us -> none
    while x2 -> x0, local copies, waits for them, and re-layouts: 10.7 us -> none  [attend(): scores = lax.fori_loop(lowest, span, fill, empty)]
  transfers between devices with their start and end apart: 6 -> 0, of which waited for: 3 -> 0; matrix products, arithmetic and copies ran while one was open for 42% -> 0% of each run, Pallas kernels for 0% -> 0%
where the time goes in v1:
time: 91.9 us; the launch traced here: 91.6 us
  Pallas kernels  80.5 us (88%)
  local copies, waits for them, and re-layouts  10.4 us (11%)
    pallas_call x1, Pallas kernels, fused(): pl.pallas_call(functools.partial(kernel, n), out_shape=(jax.ShapeDtypeStr...  80.5 us
    unnamed x12, local copies, waits for them, and re-layouts  8.8 us

profile of v1, /device:TPU:0, one launch (start us, length us, event | category | flops | bytes accessed | tf_op | source)
XLA Modules:
  0.0 91.6 jit_solution(9560972485142536149)
XLA Ops:
  0.6 0.0 copy-start.3
  0.6 0.0 copy-start.2
  0.7 0.0 copy-start.4
  0.7 0.0 copy-start.1
  0.7 0.0 copy-start
  0.7 0.8 reshape.7.gain
  1.5 6.5 %copy.10.w_down = bf16[3584,576]{1,0:T(8,128)(2,1)} copy(bf16[3584,576]{0,1:T(8,128)(2,1)} %param.9) | data formatting | bytes 8257536 | tf_op args[1]
  8.0 0.0 copy-done.3
  8.0 0.0 copy-done.2
  8.0 0.0 copy-done.4
  8.0 0.0 copy-done.1
  8.0 0.0 copy-done
  8.0 80.5 %shard_map.95 = (bf16[128,4096]{1,0:T(8,128)(2,1)}, bf16[128,576]{1,0:T(8,128)(2,1)S(1)}) custom-call(bf16[128,3584]{1,0:T(8,128)(2,1)S(1)} %copy-done, bf16[3584,576]{1,0:T(8,128)(2,1)} %copy.10.w_down, bf16[1,512]{1,0:T(2,128)(2,1)S(1)} %reshape.7.gain, bf16[128,18432]{1,0:T(8,128)(2,1)} %queries.1, bf16[32,64,128]{2,1,0:T(8,128)(2,1)S(1)} %copy-done.1, ...), custom_call_target="tpu_custom_call" | custom-call | tf_op jit(solution)/shard_map/pallas_call | solution.py:528
  88.6 0.8 copy.11
  89.3 2.3 %copy.13 = bf16[128,4096]{1,0:T(8,128)(2,1)} copy(bf16[128,4096]{1,0:T(8,128)(2,1)} %get-tuple-element.6) | data formatting | bytes 2097152
Async XLA Ops:
  0.6 7.3 %copy-start.3 = (s32[8,8]{1,0:T(8,128)S(1)}, s32[8,8]{1,0:T(8,128)}, u32[]{:S(2)}) copy-start(s32[8,8]{1,0:T(8,128)} %owners.1) | copy-start | bytes 772
  0.6 7.3 %copy-start.2 = (s32[8,8]{1,0:T(8,128)S(1)}, s32[8,8]{1,0:T(8,128)}, u32[]{:S(2)}) copy-start(s32[8,8]{1,0:T(8,128)} %migrate.1) | copy-start | bytes 772
  0.7 7.3 %copy-start.4 = (s32[4]{0:T(128)S(1)}, s32[4]{0:T(128)}, u32[]{:S(2)}) copy-start(s32[4]{0:T(128)} %prompt_blocks.1) | copy-start | bytes 52
  0.7 7.3 %copy-start.1 = (bf16[32,64,128]{2,1,0:T(8,128)(2,1)S(1)}, bf16[32,64,128]{2,1,0:T(8,128)(2,1)}, u32[]{:S(2)}) copy-start(bf16[32,64,128]{2,1,0:T(8,128)(2,1)} %w_up.1) | copy-start | bytes 1572868
  0.7 7.3 %copy-start = (bf16[128,3584]{1,0:T(8,128)(2,1)S(1)}, bf16[128,3584]{1,0:T(8,128)(2,1)}, u32[]{:S(2)}) copy-start(bf16[128,3584]{1,0:T(8,128)(2,1)} %hidden.1) | copy-start | bytes 2752516

commit v2 on v1

--- a/solution.py
+++ b/solution.py
@@ -174,11 +174,13 @@
 
 
 def kernel(
-    n, hidden, w_down, gain, queries, w_up, prompt_blocks, migrate, owners,
+    n, hidden, w_down, gain_in, queries, w_up, blocks_in, migrate_in, owners_in,
     served, store,
     hid, wd, qbuf, wall, part, part_in, key0, key1, latent, bias, out_mat, in_mat,
     send, recv, csend, crecv,
+    gain, prompt_blocks, migrate, owners, small_sem,
     hid_sem, wd_sem, q_sem, own_sem, part_sem, key_send, key_recv,
+    share_send, share_recv, c_share_send, c_share_recv,
     y_send, up_send, down_send, x_send, w_recv, send_sem, recv_sem, c_send, c_recv,
 ):
     me = lax.axis_index("ranks")
@@ -194,14 +196,25 @@
     other_x = {"groups": 1 - x}
 
     chunks = wd_sem.shape[0]
-    rows = wd.shape[0] // chunks
+    rows = wd.shape[1] // chunks
     hid_copy = pltpu.make_async_copy(hidden, hid, hid_sem)
     hid_copy.start()
     wd_copies = []
     for c in range(chunks):
         cut = pl.ds(c * rows, rows)
-        wd_copies.append(pltpu.make_async_copy(w_down.at[cut], wd.at[cut], wd_sem.at[c]))
+        wd_copies.append(
+            pltpu.make_async_copy(w_down.at[:, cut], wd.at[:, cut], wd_sem.at[c])
+        )
         wd_copies[-1].start()
+
+    small = [
+        pltpu.make_async_copy(src, dst, small_sem.at[i])
+        for i, (src, dst) in enumerate(
+            ((gain_in, gain), (blocks_in, prompt_blocks), (migrate_in, migrate), (owners_in, owners))
+        )
+    ]
+    for copy in small:
+        copy.start()
 
     barrier = pltpu.get_barrier_semaphore()
     for k in range(1, n):
@@ -210,40 +223,94 @@
     pl.semaphore_signal(barrier, 1, device_id=other_x, device_id_type=MESH)
     pl.semaphore_wait(barrier, n + 1)
 
-    def hcut(h):
-        return pl.ds(h * half, half)
-
-    def slot(r, h):
-        return wall.at[r, hcut(h)]
-
-    def hop(sems, src, r, h, where):
-        return remote(src, slot(r, h), sems.at[r, h], w_recv.at[r, h], where)
-
-    y_first = hop(y_send, w_up.at[hcut(x)], me, x, {"ranks": twin})
-    y_last = hop(y_send, w_up.at[hcut(1 - x)], me, 1 - x, {"ranks": twin})
+    quarter = half // 2
+
+    def near(r, h, other):
+        return wall.at[r, pl.ds(h * half, quarter if other else half)]
+
+    def far(r, h):
+        return wall.at[r, pl.ds(h * half + quarter, quarter)]
+
+    def own(h, other):
+        return w_up.at[pl.ds(h * half, quarter if other else half)]
+
+    def y_own(h):
+        return remote(own(h, False), near(me, h, False), y_send.at[me, h], w_recv.at[me, h, 0], {"ranks": twin})
+
+    def y_far(r, h):
+        return remote(far(r, h), far(r, h), y_send.at[r, h], w_recv.at[r, h, 1], {"ranks": twin})
+
+    def up_hop(r, src, other):
+        to = {"ranks": jnp.minimum(me + 2, n - 2 + y)}
+        return remote(src, near(r, x, other), up_send.at[r], w_recv.at[r, x, 0], to)
+
+    def down_hop(r, src, other):
+        to = {"ranks": jnp.maximum(me - 2, y)}
+        return remote(src, near(r, x, other), down_send.at[r], w_recv.at[r, x, 0], to)
+
+    def x_hop(r, other):
+        return remote(near(r, x, other), near(r, x, other), x_send.at[r], w_recv.at[r, x, 0], other_x)
+
+    def arrived(r, h, other):
+        remote(near(r, h, other), near(r, h, other), x_send.at[r], w_recv.at[r, h, 0], other_x).wait_recv()
+
     own_copy = pltpu.make_async_copy(w_up, wall.at[me], own_sem)
 
-    def up_hop(r, src):
-        return hop(up_send, src, r, x, {"ranks": jnp.minimum(me + 2, n - 2 + y)})
-
-    def down_hop(r, src):
-        return hop(down_send, src, r, x, {"ranks": jnp.maximum(me - 2, y)})
-
-    def x_hop(r):
-        return hop(x_send, slot(r, x), r, x, other_x)
-
-    def arrived(r, h):
-        remote(slot(r, h), slot(r, h), x_send.at[r, h], w_recv.at[r, h], other_x).wait_recv()
-
-    y_first.start()
+    def at_levels(d, other, act):
+        for sign, within in ((-1, z >= d), (1, z + d < levels)):
+            @pl.when(within)
+            def _():
+                level = jnp.clip(z + sign * d, 0, levels - 1)
+                act(2 * level + (1 - y if other else y), sign)
+
+    def relay(d, same):
+        other = not same
+
+        def act(r, sign):
+            arrived(r, x, other)
+            if d < levels - 1:
+                if sign < 0:
+                    @pl.when(z < levels - 1)
+                    def _():
+                        up_hop(r, near(r, x, other), other).start()
+                else:
+                    @pl.when(z > 0)
+                    def _():
+                        down_hop(r, near(r, x, other), other).start()
+
+            x_hop(r, other).start()
+            if same:
+                y_far(r, x).start()
+
+        at_levels(d, other, act)
+
+    def relay_x(d):
+        def act(r, sign):
+            arrived(r, 1 - x, False)
+            y_far(r, 1 - x).start()
+
+        at_levels(d, False, act)
+
+    def gathered(h):
+        def act(r, sign):
+            if h is None:
+                arrived(r, 1 - x, True)
+                y_far(r, 1 - x).wait_recv()
+            else:
+                y_far(r, x).wait_recv()
+
+        for d in range(1, levels):
+            at_levels(d, True, act)
+
+    y_own(x).start()
 
     @pl.when(z < levels - 1)
     def _():
-        up_hop(me, w_up.at[hcut(x)]).start()
+        up_hop(me, own(x, False), False).start()
 
     @pl.when(z > 0)
     def _():
-        down_hop(me, w_up.at[hcut(x)]).start()
+        down_hop(me, own(x, False), False).start()
 
     q_copies = []
     for parity in range(2):
@@ -257,20 +324,34 @@
             )
             q_copies[-1].start()
     own_copy.start()
-    y_last.start()
+    y_own(1 - x).start()
 
     hid_copy.wait()
     for c in range(chunks):
         wd_copies[c].wait()
-        term = jnp.dot(
+        term = lax.dot_general(
             hid[:, c * rows : (c + 1) * rows],
-            wd[c * rows : (c + 1) * rows, :],
+            wd[:, c * rows : (c + 1) * rows],
+            (((1,), (1,)), ((), ())),
             preferred_element_type=jnp.float32,
         )
         part[...] = term if c == 0 else part[...] + term
     part_copy = remote(part, part_in, part_sem.at[0], part_sem.at[1], {"tensor": 1 - core})
     part_copy.start()
 
+    arrived(twin, x, False)
+
+    @pl.when(z < levels - 1)
+    def _():
+        up_hop(twin, near(twin, x, True), True).start()
+
+    @pl.when(z > 0)
+    def _():
+        down_hop(twin, near(twin, x, True), True).start()
+
+    relay(1, True)
+    for copy in small:
+        copy.wait()
     out_mat[0] = send_matrix(migrate, me, n)
     out_mat[1] = send_matrix(owners, me, n)
     in_mat[0] = take_matrix(migrate, me, n)
@@ -289,31 +370,33 @@
     raw = part[...] + part_in[...]
     lead = raw[:, :LAT]
     mean_square = jnp.mean(lead * lead, axis=-1, keepdims=True)
-    normed = lead * lax.rsqrt(mean_square + 1e-06) * gain[...].astype(jnp.float32)
+    normed = lead * lax.rsqrt(mean_square + 1e-06) * gain[...].astype(jnp.float32).reshape(1, LAT)
     rope = raw[:, LAT:]
     blank = jnp.zeros((tok, ROPE), jnp.float32)
     key0[BLOCKS - 1] = jnp.concatenate([normed, rope, blank], axis=-1).astype(jnp.bfloat16)
 
+    my_rows = pl.ds(core * (tok // 2), tok // 2)
+    its_rows = pl.ds((1 - core) * (tok // 2), tok // 2)
+
     def key_copy(d, r):
         return remote(
-            key0.at[BLOCKS - 1], key0.at[BLOCKS - 1 - d], key_send.at[d], key_recv.at[d], {"ranks": r}
-        )
+            key0.at[BLOCKS - 1, my_rows],
+            key0.at[BLOCKS - 1 - d, my_rows],
+            key_send.at[d],
+            key_recv.at[d],
+            {"ranks": r},
+        )
+
+    def key_share(d, part_rows):
+        block = key0.at[BLOCKS - 1 - d, part_rows]
+        return remote(block, block, share_send.at[d], share_recv.at[d], {"tensor": 1 - core})
 
     for d in range(1, BLOCKS):
         @pl.when(me + d < n)
         def _():
             key_copy(d, (me + d) % n).start()
 
-    arrived(twin, x)
-
-    @pl.when(z < levels - 1)
-    def _():
-        up_hop(twin, slot(twin, x)).start()
-
-    @pl.when(z > 0)
-    def _():
-        down_hop(twin, slot(twin, x)).start()
-
+    relay(1, False)
     csend[...] = (
         jnp.dot(out_mat[1], key0[BLOCKS - 1], preferred_element_type=jnp.float32)
         .astype(jnp.bfloat16)
@@ -325,48 +408,30 @@
         to = (me + k) % n
         return remote(csend.at[to], crecv.at[me], c_send.at[to], c_recv.at[me], {"ranks": to})
 
-    for k in range(1, n):
-        c_copy(k).start()
+    @pl.when(y == core)
+    def _():
+        for k in range(1, n):
+            c_copy(k).start()
 
     for d in range(1, BLOCKS):
         @pl.when(me >= d)
         def _():
             key_copy(d, (me + d) % n).wait_recv()
+            key_share(d, my_rows).start()
 
         @pl.when(me < d)
         def _():
             key0[BLOCKS - 1 - d] = jnp.zeros((tok, WIDE), jnp.bfloat16)
 
+    for d in range(1, BLOCKS):
+        @pl.when(me >= d)
+        def _():
+            key_share(d, its_rows).wait_recv()
+
     for b in range(BLOCKS):
         key1[b] = jnp.concatenate(
             [jnp.zeros((tok, ROPE), jnp.bfloat16), key0[b][:, : LAT + ROPE]], axis=-1
         )
-
-    def relay(d, same):
-        def row(level):
-            return 2 * level + (y if same else 1 - y)
-
-        @pl.when(z >= d)
-        def _():
-            r = row(jnp.maximum(z - d, 0))
-            arrived(r, x)
-            if d < levels - 1:
-                @pl.when(z < levels - 1)
-                def _():
-                    up_hop(r, slot(r, x)).start()
-
-            x_hop(r).start()
-
-        @pl.when(z + d < levels)
-        def _():
-            r = row(jnp.minimum(z + d, levels - 1))
-            arrived(r, x)
-            if d < levels - 1:
-                @pl.when(z > 0)
-                def _():
-                    down_hop(r, slot(r, x)).start()
-
-            x_hop(r).start()
 
     factor = 2.0 / math.sqrt(LAT + ROPE) * math.log2(math.e)
     step = 4
@@ -391,23 +456,26 @@
         )
         latent[parity, at] = out.astype(jnp.bfloat16).reshape(step, tok, LAT)
 
-    events = [(d, same) for d in range(1, levels) for same in (True, False)]
-    plan = [events[:1], events[1:2], events[2:3], events[3:4], events[4:]]
+    plan = [
+        [lambda: relay(2, True), lambda: relay_x(1)],
+        [lambda: relay(2, False)],
+        [lambda: relay(3, True), lambda: relay_x(2)],
+        [lambda: relay(3, False)],
+    ]
+    last = [lambda: relay_x(3)]
     for copy in q_copies:
         copy.wait()
     spots = iter(plan)
     for parity, keys in ((0, key0), (1, key1)):
         for lower in (0, 2):
             for event in next(spots):
-                relay(*event)
+                event()
 
             def some(g, carry, parity=parity, keys=keys):
                 attend(parity, keys, g)
                 return carry
 
             lax.fori_loop(lower, lower + 2, some, 0)
-    for event in next(spots):
-        relay(*event)
 
     group = heads // GROUPS
     wide = group * w_up.shape[2]
@@ -424,6 +492,15 @@
             send_sem.at[g, to],
             recv_sem.at[g, me],
             {"ranks": to},
+        )
+
+    def piece_in(g, r):
+        return remote(
+            send.at[r, :, gcols(g)],
+            recv.at[r, :, gcols(g)],
+            send_sem.at[g, r],
+            recv_sem.at[g, r],
+            {"ranks": r},
         )
 
     def project(g):
@@ -444,76 +521,90 @@
             piece_copy(g, k).start()
         recv[me, :, gcols(g)] = send[me, :, gcols(g)]
 
+    def c_share(r):
+        return remote(crecv.at[r], crecv.at[r], c_share_send.at[r], c_share_recv.at[r], {"tensor": 1 - core})
+
+    def c_sides(side, act):
+        for j in range(n // 2):
+            r = 2 * j + side
+
+            @pl.when(r != me)
+            def _():
+                act(r)
+
+    def c_forward(r):
+        remote(csend.at[r], crecv.at[r], c_send.at[r], c_recv.at[r], {"ranks": twin}).wait_recv()
+        c_share(r).start()
+
     own_copy.wait()
+    gathered(x)
     for i in range(GROUPS // 2):
         project(x * (GROUPS // 2) + i)
-    arrived(twin, 1 - x)
-    for d in range(1, levels):
-        for same in (True, False):
-            def row(level):
-                return 2 * level + (y if same else 1 - y)
-
-            @pl.when(z >= d)
-            def _():
-                arrived(row(jnp.maximum(z - d, 0)), 1 - x)
-
-            @pl.when(z + d < levels)
-            def _():
-                arrived(row(jnp.minimum(z + d, levels - 1)), 1 - x)
-
+    c_sides(core, c_forward)
+    for event in last:
+        event()
+    arrived(twin, 1 - x, False)
+    gathered(None)
     for i in range(GROUPS // 2):
         project((1 - x) * (GROUPS // 2) + i)
 
-    for k in range(1, n):
-        r = (me + k) % n
-        remote(csend.at[r], crecv.at[r], c_send.at[r], c_recv.at[r], {"ranks": r}).wait_recv()
-    kept = jnp.dot(
-        in_mat[1], crecv[...].reshape(n * PIECE, WIDE), preferred_element_type=jnp.float32
-    )
-    store[...] = kept[:, : LAT + ROPE].astype(jnp.bfloat16)
+    c_sides(1 - core, lambda r: c_share(r).wait_recv())
+    kept = lax.dot_general(
+        crecv[...].reshape(n * PIECE, WIDE),
+        in_mat[1],
+        (((0,), (1,)), ((), ())),
+        preferred_element_type=jnp.float32,
+    )
+    store[...] = kept[: LAT + ROPE].astype(jnp.bfloat16)
     for i in range(GROUPS):
         g = (x * (GROUPS // 2) + i) % GROUPS
         for k in range(1, n):
             r = (me + k) % n
-            remote(
-                send.at[r, :, gcols(g)],
-                recv.at[r, :, gcols(g)],
-                send_sem.at[g, r],
-                recv_sem.at[g, r],
-                {"ranks": r},
-            ).wait_recv()
+            piece_in(g, r).wait_recv()
         served[:, gcols(g)] = jnp.dot(
             in_mat[0],
             recv[:, :, gcols(g)].reshape(n * PIECE, wide),
             preferred_element_type=jnp.float32,
         ).astype(jnp.bfloat16)
 
-    y_first.wait_send()
-    y_last.wait_send()
+    y_own(x).wait_send()
+    y_own(1 - x).wait_send()
     for d in range(1, BLOCKS):
         @pl.when(me + d < n)
         def _():
             key_copy(d, (me + d) % n).wait_send()
 
+        @pl.when(me >= d)
+        def _():
+            key_share(d, my_rows).wait_send()
+
+    @pl.when(y == core)
+    def _():
+        for k in range(1, n):
+            c_copy(k).wait_send()
+
+    c_sides(core, lambda r: c_share(r).wait_send())
     for k in range(1, n):
-        c_copy(k).wait_send()
         for g in range(GROUPS):
             piece_copy(g, k).wait_send()
-    for level_at in range(levels):
-        for same in (True, False):
-            r = 2 * level_at + (y if same else 1 - y)
-
-            @pl.when((z >= level_at) & (z < levels - 1))
+    for level in range(levels):
+        for other in (False, True):
+            r = 2 * level + (1 - y if other else y)
+
+            @pl.when((z >= level) & (z < levels - 1))
             def _():
-                up_hop(r, slot(r, x)).wait_send()
-
-            @pl.when((z <= level_at) & (z > 0))
+                up_hop(r, near(r, x, other), other).wait_send()
+
+            @pl.when((z <= level) & (z > 0))
             def _():
-                down_hop(r, slot(r, x)).wait_send()
-
-            @pl.when(z != level_at)
+                down_hop(r, near(r, x, other), other).wait_send()
+
+            @pl.when(z != level)
             def _():
-                x_hop(r).wait_send()
+                x_hop(r, other).wait_send()
+                if not other:
+                    y_far(r, x).wait_send()
+                    y_far(r, 1 - x).wait_send()
 
 
 def fused(hidden, w_down, latent_gain, queries, w_up_value, prompt_blocks, migrate, owners):
@@ -522,20 +613,19 @@
     heads, _, vdim = w_up_value.shape
     any_space = pl.BlockSpec(memory_space=pl.ANY)
     vmem = pl.BlockSpec(memory_space=pltpu.VMEM)
-    smem = pl.BlockSpec(memory_space=pltpu.SMEM)
     bf16 = jnp.bfloat16
     dma = pltpu.SemaphoreType.DMA
-    return pl.pallas_call(
+    served, store = pl.pallas_call(
         functools.partial(kernel, n),
         out_shape=(
             jax.ShapeDtypeStruct((tok, heads * vdim), bf16),
-            jax.ShapeDtypeStruct((tok, LAT + ROPE), bf16),
+            jax.ShapeDtypeStruct((LAT + ROPE, tok), bf16),
         ),
-        in_specs=[any_space, any_space, vmem, any_space, any_space, smem, smem, smem],
+        in_specs=[any_space] * 8,
         out_specs=(vmem, vmem),
         scratch_shapes=[
             pltpu.VMEM((tok, depth), bf16),
-            pltpu.VMEM((depth, LAT + ROPE), bf16),
+            pltpu.VMEM((LAT + ROPE, depth), bf16),
             pltpu.VMEM((2, heads // 2, tok, WIDE), bf16),
             pltpu.VMEM((n, heads, w_up_value.shape[1], vdim), bf16),
             pltpu.VMEM((tok, LAT + ROPE), jnp.float32),
@@ -550,6 +640,11 @@
             pltpu.VMEM((n, PIECE, heads * vdim), bf16),
             pltpu.VMEM((n, PIECE, WIDE), bf16),
             pltpu.VMEM((n, PIECE, WIDE), bf16),
+            pltpu.VMEM((LAT,), bf16),
+            pltpu.SMEM(prompt_blocks.shape, jnp.int32),
+            pltpu.SMEM(migrate.shape, jnp.int32),
+            pltpu.SMEM(owners.shape, jnp.int32),
+            dma((4,)),
             dma(()),
             dma((4,)),
             dma((2, heads // 2)),
@@ -557,23 +652,28 @@
             dma((2,)),
             dma((BLOCKS,)),
             dma((BLOCKS,)),
+            dma((BLOCKS,)),
+            dma((BLOCKS,)),
+            dma((n,)),
+            dma((n,)),
             dma((n, 2)),
-            dma((n, 2)),
-            dma((n, 2)),
-            dma((n, 2)),
-            dma((n, 2)),
+            dma((n,)),
+            dma((n,)),
+            dma((n,)),
+            dma((n, 2, 2)),
             dma((GROUPS, n)),
             dma((GROUPS, n)),
             dma((n,)),
             dma((n,)),
         ],
         compiler_params=pltpu.CompilerParams(
-            collective_id=0, has_side_effects=True, vmem_limit_bytes=52 * 1024 * 1024
+            collective_id=0, has_side_effects=True, vmem_limit_bytes=63 * 1024 * 1024
         ),
     )(
-        hidden, w_down, latent_gain.reshape(1, LAT), queries, w_up_value,
+        hidden, w_down.T, latent_gain, queries, w_up_value,
         prompt_blocks, migrate, owners,
     )
+    return served, store.T
 
 
 def solution(mesh):

time: 91.9 us -> 77.5 us (0.84)
  Pallas kernels: 80.5 us -> 72.8 us
  local copies, waits for them, and re-layouts: 10.4 us -> 3.87 us
    pallas_call x1, Pallas kernels: 80.5 us -> 72.8 us  [fused(): pl.pallas_call(functools.partial(kernel, n), out_shape=(jax.ShapeDtypeStr...]
    unnamed x12 -> x2, local copies, waits for them, and re-layouts: 8.8 us -> 3.87 us
where the time goes in v2:
time: 77.5 us; the launch traced here: 77.3 us
  Pallas kernels  72.8 us (94%)
  local copies, waits for them, and re-layouts  3.87 us (5%)
    pallas_call x1, Pallas kernels, fused(): pl.pallas_call(functools.partial(kernel, n), out_shape=(jax.ShapeDtypeStr...  72.8 us
    unnamed x2, local copies, waits for them, and re-layouts  3.87 us

profile of v2, /device:TPU:0, one launch (start us, length us, event | category | flops | bytes accessed | tf_op | source)
XLA Modules:
  0.0 77.3 jit_solution(8376328553014706590)
XLA Ops:
  0.6 72.8 %shard_map.95 = (bf16[128,4096]{1,0:T(8,128)(2,1)}, bf16[576,128]{1,0:T(8,128)(2,1)}) custom-call(bf16[128,3584]{1,0:T(8,128)(2,1)} %hidden.1, bf16[576,3584]{1,0:T(8,128)(2,1)} %bitcast.2, bf16[512]{0:T(512)(128)(2,1)} %gain_in.1, bf16[128,18432]{1,0:T(8,128)(2,1)} %queries.1, bf16[32,64,128]{2,1,0:T(8,128)(2,1)} %w_up.1, s32[4]{0:T(128)} %blocks_in.1, ...), custom_call_target="tpu_custom_call" | custom-call | tf_op jit(solution)/shard_map/pallas_call | solution.py:618
  73.4 2.3 %copy.12 = bf16[128,4096]{1,0:T(8,128)(2,1)} copy(bf16[128,4096]{1,0:T(8,128)(2,1)} %get-tuple-element.8) | data formatting | bytes 2097152
  75.7 1.6 %copy.13 = bf16[128,576]{0,1:T(8,128)(2,1)} copy(bf16[128,576]{0,1:T(8,128)(2,1)} %bitcast.3) | data formatting | bytes 294912

commit v3 on v2

--- a/solution.py
+++ b/solution.py
@@ -293,11 +293,7 @@
 
     def gathered(h):
         def act(r, sign):
-            if h is None:
-                arrived(r, 1 - x, True)
-                y_far(r, 1 - x).wait_recv()
-            else:
-                y_far(r, x).wait_recv()
+            y_far(r, h).wait_recv()
 
         for d in range(1, levels):
             at_levels(d, True, act)
@@ -408,11 +404,6 @@
         to = (me + k) % n
         return remote(csend.at[to], crecv.at[me], c_send.at[to], c_recv.at[me], {"ranks": to})
 
-    @pl.when(y == core)
-    def _():
-        for k in range(1, n):
-            c_copy(k).start()
-
     for d in range(1, BLOCKS):
         @pl.when(me >= d)
         def _():
@@ -457,10 +448,10 @@
         latent[parity, at] = out.astype(jnp.bfloat16).reshape(step, tok, LAT)
 
     plan = [
-        [lambda: relay(2, True), lambda: relay_x(1)],
-        [lambda: relay(2, False)],
-        [lambda: relay(3, True), lambda: relay_x(2)],
-        [lambda: relay(3, False)],
+        [lambda: relay(2, True)],
+        [lambda: relay_x(1), lambda: relay(2, False)],
+        [lambda: relay(3, True)],
+        [lambda: relay_x(2)],
     ]
     last = [lambda: relay_x(3)]
     for copy in q_copies:
@@ -536,17 +527,25 @@
         remote(csend.at[r], crecv.at[r], c_send.at[r], c_recv.at[r], {"ranks": twin}).wait_recv()
         c_share(r).start()
 
+    @pl.when(y == core)
+    def _():
+        for k in range(1, n):
+            c_copy(k).start()
+
     own_copy.wait()
-    gathered(x)
-    for i in range(GROUPS // 2):
-        project(x * (GROUPS // 2) + i)
-    c_sides(core, c_forward)
+    relay(3, False)
+    project(2 * x)
     for event in last:
         event()
+    gathered(x)
+    project(2 * x + 1)
     arrived(twin, 1 - x, False)
-    gathered(None)
-    for i in range(GROUPS // 2):
-        project((1 - x) * (GROUPS // 2) + i)
+    for d in range(1, levels):
+        at_levels(d, True, lambda r, sign: arrived(r, 1 - x, True))
+    project(2 * (1 - x))
+    gathered(1 - x)
+    project(2 * (1 - x) + 1)
+    c_sides(core, c_forward)
 
     c_sides(1 - core, lambda r: c_share(r).wait_recv())
     kept = lax.dot_general(

time: 77.5 us -> 75.2 us (0.970)
  Pallas kernels: 72.8 us -> 69.7 us
    pallas_call x1, Pallas kernels: 72.8 us -> 69.7 us  [fused(): pl.pallas_call(functools.partial(kernel, n), out_shape=(jax.ShapeDtypeStr...]
where the time goes in v3:
time: 75.2 us; the launch traced here: 74.2 us
  Pallas kernels  69.7 us (93%)
  local copies, waits for them, and re-layouts  3.87 us (5%)
    pallas_call x1, Pallas kernels, fused(): pl.pallas_call(functools.partial(kernel, n), out_shape=(jax.ShapeDtypeStr...  69.7 us
    unnamed x2, local copies, waits for them, and re-layouts  3.87 us

profile of v3, /device:TPU:0, one launch (start us, length us, event | category | flops | bytes accessed | tf_op | source)
XLA Modules:
  0.0 74.2 jit_solution(12093314630924397090)
XLA Ops:
  0.6 69.7 %shard_map.95 = (bf16[128,4096]{1,0:T(8,128)(2,1)}, bf16[576,128]{1,0:T(8,128)(2,1)}) custom-call(bf16[128,3584]{1,0:T(8,128)(2,1)} %hidden.1, bf16[576,3584]{1,0:T(8,128)(2,1)} %bitcast.2, bf16[512]{0:T(512)(128)(2,1)} %gain_in.1, bf16[128,18432]{1,0:T(8,128)(2,1)} %queries.1, bf16[32,64,128]{2,1,0:T(8,128)(2,1)} %w_up.1, s32[4]{0:T(128)} %blocks_in.1, ...), custom_call_target="tpu_custom_call" | custom-call | tf_op jit(solution)/shard_map/pallas_call | solution.py:617
  70.4 2.3 %copy.12 = bf16[128,4096]{1,0:T(8,128)(2,1)} copy(bf16[128,4096]{1,0:T(8,128)(2,1)} %get-tuple-element.8) | data formatting | bytes 2097152
  72.7 1.6 %copy.13 = bf16[128,576]{0,1:T(8,128)(2,1)} copy(bf16[128,576]{0,1:T(8,128)(2,1)} %bitcast.3) | data formatting | bytes 294912
